TPU v7x, 256 devices: a whole 4x4x8 slice. The times are simulated.
256 devices in a mesh: ta: 8 (over z), gz: 4 (over y), xy: 8 (over x, core).
Axes of the slice: x: 4, y: 4, z: 8, core: 2. Of those that a mesh axis runs over, the one named last changes fastest.
Arguments:
- right_side: float32 [2, 4, 3, 32, 16, 1024], P(None, None, None, 'ta', 'gz', 'xy'), may hold values from -6 to 6
- links: bfloat16 [4, 2, 3, 3, 32, 16, 1024], P(None, None, None, None, 'ta', 'gz', 'xy'), may hold values from -3.5 to 3.5
- clover_inverse: bfloat16 [2, 2, 6, 6, 32, 16, 1024], P(None, None, None, None, 'ta', 'gz', 'xy'), may hold values from -0.296875 to 1
- near_null: bfloat16 [8, 4, 8, 16, 12, 2, 4, 3, 256], P('ta', 'gz', 'xy'), may hold values from -6 to 6
- owners: int32 [8, 4, 8, 8], P('ta', 'gz', 'xy'), may hold values from 0 to 7, as said below
Outputs:
- smoothed: float32 [2, 4, 3, 32, 16, 1024], P(None, None, None, 'ta', 'gz', 'xy')
- coarse: float32 [8, 4, 8, 16, 2, 2, 12], P('ta', 'gz', 'xy')
Inputs may be any that keep to these rules, and one draw needn't show every extreme that they name: `owners`: each device assigns at most 2 of its aggregates to any one owner; in every group of devices that share ta and gz, one owner receives exactly 2 aggregates from every device of the group.
All inputs are finite; a program needn't handle non-finite values.
Results may differ from a plain program's by a relative error of at most 0.0029.
Values may be sent and summed in bfloat16 or wider, within the bound.
A program may use at most 256 MiB of HBM per device.

v0:
```python
import jax
import jax.numpy as jnp
from jax import lax
from jax.experimental import pallas as pl
from jax.experimental.pallas import tpu as pltpu
from jax.sharding import PartitionSpec as P

LY = 32
SWEEPS = 3
MOST = 2
AGGS = 8
NV = 12
HOPPING = 0.13
F32 = jnp.float32
BF16 = jnp.bfloat16
MESH = pl.DeviceIdType.MESH
WIDTH, HEIGHT, DEPTH, TIME = range(4)
CROSSING = ((TIME, "ta"), (DEPTH, "gz"), (WIDTH, "xy"))
UPPER = {
    WIDTH: ((1, 3), (0, 3)),
    HEIGHT: ((1, 2), (0, 0)),
    DEPTH: ((0, 3), (1, 1)),
    TIME: ((0, 0), (1, 0)),
}
LOWER = {
    WIDTH: ((1, 1), (0, 1)),
    HEIGHT: ((1, 0), (0, 2)),
    DEPTH: ((0, 1), (1, 3)),
    TIME: ((0, 0), (1, 0)),
}


def roll(value, shift, axis):
    size = value.shape[axis]
    shift = shift % size
    return value if shift == 0 else pltpu.roll(value, shift, axis)


def add_phase(base, pair, power, sign):
    if sign < 0:
        power = power + 2
    real, imaginary = pair
    turned = ((real, 1), (imaginary, 1)), ((imaginary, -1), (real, 1)), ((real, -1), (imaginary, -1)), ((imaginary, 1), (real, -1))
    out = []
    for part, (value, factor) in zip(base, turned[power % 4]):
        out.append(part + value if factor > 0 else part - value)
    return tuple(out)


def project(load, mu, sign):
    half = []
    for spin in range(2):
        source, power = UPPER[mu][spin]
        half.append([
            add_phase(load(spin, color), load(2 + source, color), power, sign)
            for color in range(3)
        ])
    return half


def color_row(link, vector, row, adjoint):
    real = imaginary = None
    for column in range(3):
        at = (column, row) if adjoint else (row, column)
        link_real, link_imaginary = link(0, *at), link(1, *at)
        vector_real, vector_imaginary = vector[column]
        first, second = link_real * vector_real, link_real * vector_imaginary
        third, fourth = link_imaginary * vector_imaginary, link_imaginary * vector_real
        if adjoint:
            first, second = first + third, second - fourth
        else:
            first, second = first - third, second + fourth
        real = first if real is None else real + first
        imaginary = second if imaginary is None else imaginary + second
    return real, imaginary


def kernel(rs_hbm, links_hbm, clover_hbm, near_hbm, owners, smoothed_hbm, coarse,
           rs, links16, clover, near, links, face_links, field, smooth, acc,
           outbox, inbox, tiles, placing, parcels, arrived, sums,
           load_sem, store_sem, send_sem, recv_sem, parcel_send, parcel_recv):
    groups = lax.axis_size("xy")
    slots = groups * MOST
    me = {axis: lax.axis_index(axis) for axis in ("ta", "gz", "xy")}

    def shifted(axis, offset):
        size = lax.axis_size(axis)
        return lax.rem(me[axis] + (offset + size), size)

    loads = [
        pltpu.make_async_copy(source, target, load_sem.at[i])
        for i, (source, target) in enumerate(
            ((rs_hbm, rs), (clover_hbm, clover), (links_hbm, links16), (near_hbm, near))
        )
    ]
    for copy in loads:
        copy.start()

    barrier = pltpu.get_barrier_semaphore()
    greeted = 0
    for axis in ("ta", "gz"):
        for offset in (1, -1):
            pl.semaphore_signal(barrier, inc=1, device_id={axis: shifted(axis, offset)}, device_id_type=MESH)
            greeted += 1
    for offset in range(1, groups):
        pl.semaphore_signal(barrier, inc=1, device_id={"xy": shifted("xy", offset)}, device_id_type=MESH)
        greeted += 1

    row8 = lax.broadcasted_iota(jnp.int32, (8, 128), 0)
    lane8 = lax.broadcasted_iota(jnp.int32, (8, 128), 1)
    upper_rows = row8 >= 4
    depth_at = row8 % 4
    width_at = lane8 // LY
    height_at = lane8 % LY

    def pack(values, mu, high):
        if mu == TIME:
            if high:
                return jnp.where(upper_rows, values[1][1], roll(values[0][1], 4, 0))
            return jnp.where(upper_rows, roll(values[1][0], 4, 0), values[0][0])
        axis, unit, at = (0, 1, depth_at) if mu == DEPTH else (1, LY, width_at)
        face = 3 if high else 0
        out = None
        for index in range(4):
            piece = roll(values[index // 2][index % 2], (index - face) * unit, axis)
            out = piece if out is None else jnp.where(at == index, piece, out)
        return out

    def unpack(packed, mu, high):
        if mu == TIME:
            if high:
                return [
                    (None, jnp.where(upper_rows, roll(packed, 4 * (1 - spin), 0), 0.0))
                    for spin in range(2)
                ]
            return [
                (jnp.where(upper_rows, 0.0, roll(packed, 4 * spin, 0)), None)
                for spin in range(2)
            ]
        axis, unit, at = (0, 1, depth_at) if mu == DEPTH else (1, LY, width_at)
        face = 3 if high else 0
        pieces = [
            jnp.where(at == face, roll(packed, (face - index) * unit, axis), 0.0)
            for index in range(4)
        ]
        return [(pieces[2 * spin], pieces[2 * spin + 1]) for spin in range(2)]

    def neighbour(value, mu, ahead):
        if mu == HEIGHT:
            step = -1 if ahead else 1
            edge = height_at == (LY - 1 if ahead else 0)
            return jnp.where(edge[None], roll(value, -step * (LY - 1), 2), roll(value, step, 2))
        if mu == TIME:
            turned = roll(value, 4, 1)
            if ahead:
                first = jnp.where(upper_rows, turned[1], turned[0])
                second = jnp.where(upper_rows, 0.0, turned[1])
            else:
                first = jnp.where(upper_rows, turned[0], 0.0)
                second = jnp.where(upper_rows, turned[1], turned[0])
            return jnp.stack([first, second])
        axis, unit, at = (1, 1, depth_at) if mu == DEPTH else (2, LY, width_at)
        edge = at == (3 if ahead else 0)
        return jnp.where(edge[None], 0.0, roll(value, -unit if ahead else unit, axis))

    def component(part, spin, color):
        return (part * 4 + spin) * 3 + color

    def load_field(spin, color):
        return field[component(0, spin, color)], field[component(1, spin, color)]

    def message(sweep, way, axis, offset):
        return pltpu.make_async_remote_copy(
            src_ref=outbox.at[sweep, way],
            dst_ref=inbox.at[sweep, way],
            send_sem=send_sem.at[sweep, way],
            recv_sem=recv_sem.at[sweep, way],
            device_id={axis: shifted(axis, offset)},
            device_id_type=MESH,
        )

    acc[...] = jnp.zeros(acc.shape, F32)
    smooth[...] = jnp.zeros(smooth.shape, F32)
    sums[...] = jnp.zeros(sums.shape, F32)

    owner = [owners[i] for i in range(AGGS)]
    target = []
    for i in range(AGGS):
        rank = jnp.int32(0)
        for j in range(i):
            rank = rank + jnp.where(owner[j] == owner[i], 1, 0)
        target.append(owner[i] * MOST + rank)
    lane_from = lax.broadcasted_iota(jnp.int32, (128, 128), 0)
    lane_to = lax.broadcasted_iota(jnp.int32, (128, 128), 1)
    slot_of = jnp.zeros((128, 128), jnp.int32)
    for i in range(AGGS):
        slot_of = jnp.where((lane_from // 4) % AGGS == i, target[i], slot_of)
    same_site = (lane_from // LY) * 4 + lane_from % 4 == lane_to % 16
    for part in range(slots // 8):
        placing[:, part * 128:(part + 1) * 128] = jnp.where(
            same_site & (slot_of == lane_to // 16 + part * 8), 1.0, 0.0
        ).astype(BF16)

    loads[0].wait()
    loads[1].wait()

    def body(sweep, carry):
        kept = jnp.where(sweep == SWEEPS - 1, 1.0, 0.0)
        for chirality in range(2):
            vector = [
                [rs[component(part, 2 * chirality, j)] + HOPPING * acc[component(part, 2 * chirality, j)]
                 for part in range(2)]
                for j in range(6)
            ]
            for i in range(6):
                real = imaginary = None
                for j in range(6):
                    block_real = clover[chirality, 0, i * 6 + j].astype(F32).reshape(2, 8, 128)
                    block_imaginary = clover[chirality, 1, i * 6 + j].astype(F32).reshape(2, 8, 128)
                    first = block_real * vector[j][0] - block_imaginary * vector[j][1]
                    second = block_real * vector[j][1] + block_imaginary * vector[j][0]
                    real = first if real is None else real + first
                    imaginary = second if imaginary is None else imaginary + second
                for part, value in enumerate((real, imaginary)):
                    at = component(part, 2 * chirality, i)
                    field[at] = value - kept * smooth[at]
                    smooth[at] = value

        @pl.when(sweep == SWEEPS - 1)
        def _():
            pltpu.make_async_copy(smooth, smoothed_hbm, store_sem).start()

        @pl.when(sweep == 0)
        def _():
            loads[2].wait()
            for mu in range(4):
                for part in range(2):
                    for at in range(9):
                        links[mu, part, at] = links16[mu, part, at].astype(F32).reshape(2, 8, 128)
            for order, (mu, _) in enumerate(CROSSING):
                for part in range(2):
                    for at in range(9):
                        value = links[mu, part, at]
                        face_links[order, part, at] = pack([value, value], mu, True)
            pl.semaphore_wait(barrier, greeted)

        for order, (mu, axis) in enumerate(CROSSING):
            half = project(load_field, mu, -1)
            for part in range(2):
                for color in range(3):
                    outbox[sweep, 2 * order, part * 3 + color] = pack(
                        [half[0][color][part], half[1][color][part]], mu, False)
            message(sweep, 2 * order, axis, -1).start()
        for order, (mu, axis) in enumerate(CROSSING):
            half = project(load_field, mu, 1)
            packed = [
                tuple(pack([half[0][color][part], half[1][color][part]], mu, True) for part in range(2))
                for color in range(3)
            ]

            def face_link(part, row, column, order=order):
                return face_links[order, part, row * 3 + column]

            for row in range(3):
                pair = color_row(face_link, packed, row, True)
                for part in range(2):
                    outbox[sweep, 2 * order + 1, part * 3 + row] = pair[part]
            message(sweep, 2 * order + 1, axis, 1).start()

        started = False
        for mu in (HEIGHT, TIME, DEPTH, WIDTH):
            def link(part, row, column, mu=mu):
                return links[mu, part, row * 3 + column]

            for sign in (-1, 1):
                half = project(load_field, mu, sign)
                if sign < 0:
                    half = [[tuple(neighbour(value, mu, True) for value in pair) for pair in spin] for spin in half]
                for row in range(3):
                    moved = []
                    for spin in range(2):
                        pair = color_row(link, half[spin], row, sign > 0)
                        if sign > 0:
                            pair = tuple(neighbour(value, mu, False) for value in pair)
                        moved.append(pair)
                    for spin in range(4):
                        places = [component(part, spin, row) for part in range(2)]
                        base = tuple(acc[at] for at in places) if started else (0.0, 0.0)
                        if spin < 2:
                            total = add_phase(base, moved[spin], 0, 1)
                        else:
                            source, power = LOWER[mu][spin - 2]
                            total = add_phase(base, moved[source], power, sign)
                        for at, value in zip(places, total):
                            acc[at] = value
                started = True

        for order, (mu, axis) in enumerate(CROSSING):
            message(sweep, 2 * order, axis, -1).wait_recv()
            message(sweep, 2 * order + 1, axis, 1).wait_recv()
        for row in range(3):
            totals = [
                [[acc[component(part, spin, row), side] for side in range(2)] for part in range(2)]
                for spin in range(4)
            ]
            for order, (mu, axis) in enumerate(CROSSING):
                def face_link(part, at_row, column, order=order):
                    return face_links[order, part, at_row * 3 + column]

                for sign in (-1, 1):
                    way = 2 * order + (0 if sign < 0 else 1)
                    if sign < 0:
                        packed = [
                            (inbox[sweep, way, color], inbox[sweep, way, 3 + color]) for color in range(3)
                        ]
                        pair = color_row(face_link, packed, row, False)
                    else:
                        pair = inbox[sweep, way, row], inbox[sweep, way, 3 + row]
                    spread = [unpack(value, mu, sign < 0) for value in pair]
                    for side in range(2):
                        if spread[0][0][side] is None:
                            continue
                        pieces = [(spread[0][spin][side], spread[1][spin][side]) for spin in range(2)]
                        for spin in range(4):
                            base = totals[spin][0][side], totals[spin][1][side]
                            if spin < 2:
                                total = add_phase(base, pieces[spin], 0, 1)
                            else:
                                source, power = LOWER[mu][spin - 2]
                                total = add_phase(base, pieces[source], power, sign)
                            totals[spin][0][side], totals[spin][1][side] = total
            for spin in range(4):
                for part in range(2):
                    for side in range(2):
                        acc[component(part, spin, row), side] = totals[spin][part][side]
        return carry

    lax.fori_loop(0, SWEEPS, body, 0)

    for part in range(2):
        for color in range(3):
            for spin in range(4):
                value = HOPPING * acc[component(part, spin, color)]
                for side in range(2):
                    at = ((part * 3 + color) * 2 + side) * 4 + spin
                    tiles[at * 8:(at + 1) * 8, :] = value[side]
    rows = jnp.concatenate([tiles[pl.ds(r, 48, stride=8), :] for r in range(8)], axis=0).astype(BF16)
    placed = jnp.dot(rows, placing[...], preferred_element_type=F32)
    for part in range(slots // 8):
        parts = [placed[r * 48:(r + 1) * 48, part * 128:(part + 1) * 128] for r in range(8)]
        lane = lax.broadcasted_iota(jnp.int32, (48, 128), 1) // 16
        for step in (1, 2, 4):
            for r in range(8):
                if r & step:
                    continue
                first, second = parts[r], parts[r + step]
                odd = (lane & step) != 0
                parts[r] = jnp.where(odd, roll(second, step * 16, 1), first)
                parts[r + step] = jnp.where(odd, second, roll(first, -step * 16, 1))
        for r in range(8):
            slot = part * 8 + r
            parcels[slot // MOST, slot % MOST] = parts[r].astype(BF16)

    def parcel(offset):
        return pltpu.make_async_remote_copy(
            src_ref=parcels.at[shifted("xy", offset)],
            dst_ref=arrived.at[offset],
            send_sem=parcel_send.at[offset],
            recv_sem=parcel_recv.at[offset],
            device_id={"xy": shifted("xy", offset)},
            device_id_type=MESH,
        )

    for offset in sorted(range(1, groups), key=lambda o: -min(o, groups - o)):
        parcel(offset).start()
    arrived[0] = parcels[me["xy"]]
    loads[3].wait()

    def contract(index, carry):
        half = (index + 1) // 2
        offset = jnp.where(index % 2 == 1, half, lax.rem(groups - half, groups))

        @pl.when(index > 0)
        def _():
            parcel(offset).wait_recv()

        source = lax.rem(me["xy"] - offset + groups, groups)
        for m in range(MOST):
            slot = source * MOST + m
            tile = arrived[offset, m].astype(F32).reshape(6, 8, 128)
            turned = jnp.concatenate([tile[3:], -tile[:3]], axis=0)
            for v in range(NV):
                vector = near[slot * NV + v].astype(F32).reshape(6, 8, 128)
                for part, other in enumerate((tile, turned)):
                    total = jnp.sum(jnp.sum(vector * other, axis=0), axis=1, keepdims=True)
                    sums[v * 2 + part] = jnp.where(lane8 == slot, total, sums[v * 2 + part])
        return carry

    lax.fori_loop(0, groups, contract, 0)
    total = sums[...]
    total = total + roll(total, 4, 1)
    total = total + roll(total, -1, 1)
    total = total.reshape(NV, 2, 8, 128)
    for chirality in range(2):
        coarse[chirality] = total[:, :, 2 * chirality, :slots]

    for sweep in range(SWEEPS):
        for order, (mu, axis) in enumerate(CROSSING):
            message(sweep, 2 * order, axis, -1).wait_send()
            message(sweep, 2 * order + 1, axis, 1).wait_send()
    for offset in range(1, groups):
        parcel(offset).wait_send()
    pltpu.make_async_copy(smooth, smoothed_hbm, store_sem).wait()


def shards(right_side, links, clover_inverse, near_null, owners):
    groups = lax.axis_size("xy")
    slots = groups * MOST
    near = jnp.transpose(near_null[0, 0, 0], (0, 1, 2, 4, 3, 5)).reshape(slots, NV, 2, 3, 4, 2, 128)
    near = jnp.transpose(near, (0, 1, 2, 3, 5, 4, 6)).reshape(slots * NV, 48, 128)
    anywhere = pl.BlockSpec(memory_space=pl.ANY)
    vmem = pltpu.VMEM
    smoothed, coarse = pl.pallas_call(
        kernel,
        out_shape=(
            jax.ShapeDtypeStruct((24, 2, 8, 128), F32),
            jax.ShapeDtypeStruct((2, NV, 2, slots), F32),
        ),
        in_specs=[anywhere] * 4 + [pl.BlockSpec(memory_space=pltpu.SMEM)],
        out_specs=(anywhere, pl.BlockSpec(memory_space=vmem)),
        scratch_shapes=[
            vmem((24, 2, 8, 128), F32),
            vmem((4, 2, 9, 16, 128), BF16),
            vmem((2, 2, 36, 16, 128), BF16),
            vmem((slots * NV, 48, 128), BF16),
            vmem((4, 2, 9, 2, 8, 128), F32),
            vmem((3, 2, 9, 8, 128), F32),
            vmem((24, 2, 8, 128), F32),
            vmem((24, 2, 8, 128), F32),
            vmem((24, 2, 8, 128), F32),
            vmem((SWEEPS, 6, 6, 8, 128), F32),
            vmem((SWEEPS, 6, 6, 8, 128), F32),
            vmem((384, 128), F32),
            vmem((128, slots * 16), BF16),
            vmem((groups, MOST, 48, 128), BF16),
            vmem((groups, MOST, 48, 128), BF16),
            vmem((NV * 2, 8, 128), F32),
            pltpu.SemaphoreType.DMA((4,)),
            pltpu.SemaphoreType.DMA,
            pltpu.SemaphoreType.DMA((SWEEPS, 6)),
            pltpu.SemaphoreType.DMA((SWEEPS, 6)),
            pltpu.SemaphoreType.DMA((groups,)),
            pltpu.SemaphoreType.DMA((groups,)),
        ],
        compiler_params=pltpu.CompilerParams(
            collective_id=0, has_side_effects=True, vmem_limit_bytes=62 * 1024 * 1024
        ),
        name="smooth_and_restrict",
    )(
        right_side.reshape(24, 2, 8, 128),
        links.reshape(4, 2, 9, 16, 128),
        clover_inverse.reshape(2, 2, 36, 16, 128),
        near,
        owners.reshape(-1),
    )
    coarse = jnp.transpose(coarse, (3, 0, 2, 1))[None, None, None]
    return smoothed.reshape(2, 4, 3, 4, 4, 128), coarse


def solution(mesh):
    placed = (
        P(None, None, None, "ta", "gz", "xy"),
        P(None, None, None, None, "ta", "gz", "xy"),
        P(None, None, None, None, "ta", "gz", "xy"),
        P("ta", "gz", "xy", None, None, None, None, None, None),
        P("ta", "gz", "xy", None),
    )
    return jax.shard_map(
        shards,
        mesh=mesh,
        in_specs=placed,
        out_specs=(
            P(None, None, None, "ta", "gz", "xy"),
            P("ta", "gz", "xy", None, None, None, None),
        ),
        check_vma=False,
    )
```

profile of v0, /device:TPU:1, one launch (start us, length us, event | category | flops | bytes accessed | tf_op | source)
XLA Modules:
  0.0 31.3 jit_solution(1135774005213039941)
XLA Ops:
  0.6 27.7 %smooth_and_restrict.1 = (f32[24,2,8,128]{3,2,1,0:T(8,128)}, f32[2,12,2,16]{3,2,1,0:T(2,128)}) custom-call(f32[24,2,8,128]{3,2,1,0:T(8,128)} %bitcast.20, bf16[4,2,9,16,128]{4,3,2,1,0:T(8,128)(2,1)} %bitcast.19, bf16[2,2,36,16,128]{4,3,2,1,0:T(8,128)(2,1)} %bitcast.18, bf16[192,48,128]{2,1,0:T(8,128)(2,1)} %bitcast.17, s32[8]{0:T(128)} %bitcast.23), custom_call_target="tpu_custom_call" | custom-call | tf_op jit(solution)/shard_map/smooth_and_restrict/pallas_call | solution.py:423
  28.3 1.6 %copy.10 = f32[2,4,3,4,4,128]{5,4,3,2,1,0:T(4,128)} copy(f32[2,4,3,4,4,128]{5,4,3,2,1,0:T(4,128)} %bitcast.21) | data formatting | bytes 393216
  29.9 1.3 %copy.11 = f32[1,1,1,16,2,2,12]{3,5,6,4,2,1,0:T(2,128)} copy(f32[1,1,1,16,2,2,12]{3,5,6,4,2,1,0:T(2,128)} %bitcast.22) | data formatting | bytes 6144
where the time goes:
time: 31.4 us; the launch traced here: 31.3 us
  Pallas kernels  27.7 us (88%)
  local copies, waits for them, and re-layouts  2.96 us (9%)
  between operations  0.64 us (2%)
    pallas_call x1, Pallas kernels, shards(): pl.pallas_call(kernel, out_shape=(jax.ShapeDtypeStruct((24, 2, 8, 128), F...  27.7 us
    unnamed x2, local copies, waits for them, and re-layouts  2.96 us

commit v1 on v0

--- a/solution.py
+++ b/solution.py
@@ -75,10 +75,10 @@
     return real, imaginary
 
 
-def kernel(rs_hbm, links_hbm, clover_hbm, near_hbm, owners, smoothed_hbm, coarse,
-           rs, links16, clover, near, links, face_links, field, smooth, acc,
-           outbox, inbox, tiles, placing, parcels, arrived, sums,
-           load_sem, store_sem, send_sem, recv_sem, parcel_send, parcel_recv):
+def kernel(rs_hbm, links_hbm, clover_hbm, near_hbm, owners_hbm, smooth, sums,
+           rs, links16, clover, near, owners, links, face_links, field, acc,
+           outbox, inbox, tiles, placing, parcels, arrived,
+           load_sem, send_sem, recv_sem, parcel_send, parcel_recv):
     groups = lax.axis_size("xy")
     slots = groups * MOST
     me = {axis: lax.axis_index(axis) for axis in ("ta", "gz", "xy")}
@@ -90,10 +90,10 @@
     loads = [
         pltpu.make_async_copy(source, target, load_sem.at[i])
         for i, (source, target) in enumerate(
-            ((rs_hbm, rs), (clover_hbm, clover), (links_hbm, links16), (near_hbm, near))
+            ((rs_hbm, rs), (clover_hbm, clover), (links_hbm, links16), (near_hbm, near), (owners_hbm, owners))
         )
     ]
-    for copy in loads:
+    for copy in loads[:3] + loads[4:]:
         copy.start()
 
     barrier = pltpu.get_barrier_semaphore()
@@ -182,24 +182,6 @@
     acc[...] = jnp.zeros(acc.shape, F32)
     smooth[...] = jnp.zeros(smooth.shape, F32)
     sums[...] = jnp.zeros(sums.shape, F32)
-
-    owner = [owners[i] for i in range(AGGS)]
-    target = []
-    for i in range(AGGS):
-        rank = jnp.int32(0)
-        for j in range(i):
-            rank = rank + jnp.where(owner[j] == owner[i], 1, 0)
-        target.append(owner[i] * MOST + rank)
-    lane_from = lax.broadcasted_iota(jnp.int32, (128, 128), 0)
-    lane_to = lax.broadcasted_iota(jnp.int32, (128, 128), 1)
-    slot_of = jnp.zeros((128, 128), jnp.int32)
-    for i in range(AGGS):
-        slot_of = jnp.where((lane_from // 4) % AGGS == i, target[i], slot_of)
-    same_site = (lane_from // LY) * 4 + lane_from % 4 == lane_to % 16
-    for part in range(slots // 8):
-        placing[:, part * 128:(part + 1) * 128] = jnp.where(
-            same_site & (slot_of == lane_to // 16 + part * 8), 1.0, 0.0
-        ).astype(BF16)
 
     loads[0].wait()
     loads[1].wait()
@@ -226,21 +208,13 @@
                     field[at] = value - kept * smooth[at]
                     smooth[at] = value
 
-        @pl.when(sweep == SWEEPS - 1)
-        def _():
-            pltpu.make_async_copy(smooth, smoothed_hbm, store_sem).start()
-
         @pl.when(sweep == 0)
         def _():
             loads[2].wait()
-            for mu in range(4):
-                for part in range(2):
-                    for at in range(9):
-                        links[mu, part, at] = links16[mu, part, at].astype(F32).reshape(2, 8, 128)
             for order, (mu, _) in enumerate(CROSSING):
                 for part in range(2):
                     for at in range(9):
-                        value = links[mu, part, at]
+                        value = links16[mu, part, at].astype(F32).reshape(2, 8, 128)
                         face_links[order, part, at] = pack([value, value], mu, True)
             pl.semaphore_wait(barrier, greeted)
 
@@ -266,6 +240,32 @@
                 for part in range(2):
                     outbox[sweep, 2 * order + 1, part * 3 + row] = pair[part]
             message(sweep, 2 * order + 1, axis, 1).start()
+
+        @pl.when(sweep == 0)
+        def _():
+            loads[3].start()
+            loads[4].wait()
+            owner = [owners[i] for i in range(AGGS)]
+            target = []
+            for i in range(AGGS):
+                rank = jnp.int32(0)
+                for j in range(i):
+                    rank = rank + jnp.where(owner[j] == owner[i], 1, 0)
+                target.append(owner[i] * MOST + rank)
+            lane_from = lax.broadcasted_iota(jnp.int32, (128, 128), 0)
+            lane_to = lax.broadcasted_iota(jnp.int32, (128, 128), 1)
+            slot_of = jnp.zeros((128, 128), jnp.int32)
+            for i in range(AGGS):
+                slot_of = jnp.where((lane_from // 4) % AGGS == i, target[i], slot_of)
+            same_site = (lane_from // LY) * 4 + lane_from % 4 == lane_to % 16
+            for part in range(slots // 8):
+                placing[:, part * 128:(part + 1) * 128] = jnp.where(
+                    same_site & (slot_of == lane_to // 16 + part * 8), 1.0, 0.0
+                ).astype(BF16)
+            for mu in range(4):
+                for part in range(2):
+                    for at in range(9):
+                        links[mu, part, at] = links16[mu, part, at].astype(F32).reshape(2, 8, 128)
 
         started = False
         for mu in (HEIGHT, TIME, DEPTH, WIDTH):
@@ -397,20 +397,28 @@
         return carry
 
     lax.fori_loop(0, groups, contract, 0)
-    total = sums[...]
-    total = total + roll(total, 4, 1)
-    total = total + roll(total, -1, 1)
-    total = total.reshape(NV, 2, 8, 128)
-    for chirality in range(2):
-        coarse[chirality] = total[:, :, 2 * chirality, :slots]
-
     for sweep in range(SWEEPS):
         for order, (mu, axis) in enumerate(CROSSING):
             message(sweep, 2 * order, axis, -1).wait_send()
             message(sweep, 2 * order + 1, axis, 1).wait_send()
     for offset in range(1, groups):
         parcel(offset).wait_send()
-    pltpu.make_async_copy(smooth, smoothed_hbm, store_sem).wait()
+
+
+def finish(smooth, sums, smoothed, coarse, staged, sems):
+    first = pltpu.make_async_copy(smooth, smoothed, sems.at[0])
+    first.start()
+    slots = coarse.shape[-1]
+    total = sums[...]
+    total = total + roll(total, 4, 1)
+    total = total + roll(total, -1, 1)
+    total = total.reshape(NV, 2, 8, 128)
+    for chirality in range(2):
+        staged[chirality] = total[:, :, 2 * chirality, :slots]
+    second = pltpu.make_async_copy(staged, coarse, sems.at[1])
+    second.start()
+    first.wait()
+    second.wait()
 
 
 def shards(right_side, links, clover_inverse, near_null, owners):
@@ -420,22 +428,30 @@
     near = jnp.transpose(near, (0, 1, 2, 3, 5, 4, 6)).reshape(slots * NV, 48, 128)
     anywhere = pl.BlockSpec(memory_space=pl.ANY)
     vmem = pltpu.VMEM
-    smoothed, coarse = pl.pallas_call(
+    inside = pl.BlockSpec(memory_space=vmem)
+    operands = [
+        pltpu.with_memory_space_constraint(value, pltpu.HBM)
+        for value in (
+            right_side.reshape(24, 2, 8, 128),
+            links.reshape(4, 2, 9, 16, 128),
+            clover_inverse.reshape(2, 2, 36, 16, 128),
+            near,
+            owners.reshape(-1),
+        )
+    ]
+    smooth, sums = pl.pallas_call(
         kernel,
-        out_shape=(
-            jax.ShapeDtypeStruct((24, 2, 8, 128), F32),
-            jax.ShapeDtypeStruct((2, NV, 2, slots), F32),
-        ),
-        in_specs=[anywhere] * 4 + [pl.BlockSpec(memory_space=pltpu.SMEM)],
-        out_specs=(anywhere, pl.BlockSpec(memory_space=vmem)),
+        out_shape=(vmem((24, 2, 8, 128), F32), vmem((NV * 2, 8, 128), F32)),
+        in_specs=[anywhere] * 5,
+        out_specs=(inside, inside),
         scratch_shapes=[
             vmem((24, 2, 8, 128), F32),
             vmem((4, 2, 9, 16, 128), BF16),
             vmem((2, 2, 36, 16, 128), BF16),
             vmem((slots * NV, 48, 128), BF16),
+            pltpu.SMEM((AGGS,), jnp.int32),
             vmem((4, 2, 9, 2, 8, 128), F32),
             vmem((3, 2, 9, 8, 128), F32),
-            vmem((24, 2, 8, 128), F32),
             vmem((24, 2, 8, 128), F32),
             vmem((24, 2, 8, 128), F32),
             vmem((SWEEPS, 6, 6, 8, 128), F32),
@@ -444,25 +460,29 @@
             vmem((128, slots * 16), BF16),
             vmem((groups, MOST, 48, 128), BF16),
             vmem((groups, MOST, 48, 128), BF16),
-            vmem((NV * 2, 8, 128), F32),
-            pltpu.SemaphoreType.DMA((4,)),
-            pltpu.SemaphoreType.DMA,
+            pltpu.SemaphoreType.DMA((5,)),
             pltpu.SemaphoreType.DMA((SWEEPS, 6)),
             pltpu.SemaphoreType.DMA((SWEEPS, 6)),
             pltpu.SemaphoreType.DMA((groups,)),
             pltpu.SemaphoreType.DMA((groups,)),
         ],
         compiler_params=pltpu.CompilerParams(
-            collective_id=0, has_side_effects=True, vmem_limit_bytes=62 * 1024 * 1024
+            collective_id=0, has_side_effects=True, vmem_limit_bytes=32 * 1024 * 1024
         ),
         name="smooth_and_restrict",
-    )(
-        right_side.reshape(24, 2, 8, 128),
-        links.reshape(4, 2, 9, 16, 128),
-        clover_inverse.reshape(2, 2, 36, 16, 128),
-        near,
-        owners.reshape(-1),
-    )
+    )(*operands)
+    smoothed, coarse = pl.pallas_call(
+        finish,
+        out_shape=(
+            jax.ShapeDtypeStruct((24, 2, 8, 128), F32),
+            jax.ShapeDtypeStruct((2, NV, 2, slots), F32),
+        ),
+        in_specs=[anywhere, inside],
+        out_specs=(anywhere, anywhere),
+        scratch_shapes=[vmem((2, NV, 2, slots), F32), pltpu.SemaphoreType.DMA((2,))],
+        compiler_params=pltpu.CompilerParams(vmem_limit_bytes=32 * 1024 * 1024),
+        name="finish",
+    )(smooth, sums)
     coarse = jnp.transpose(coarse, (3, 0, 2, 1))[None, None, None]
     return smoothed.reshape(2, 4, 3, 4, 4, 128), coarse
 

time: 31.4 us -> 27.8 us (0.89)
  local copies, waits for them, and re-layouts: 2.96 us -> 0 us
  Pallas kernels: 27.7 us -> 27.1 us
    unnamed x2 -> x0, local copies, waits for them, and re-layouts: 2.96 us -> none
    pallas_call x1 -> x2, Pallas kernels: 27.7 us -> 27.1 us  [the longest x1 26.4 us: shards(): pl.pallas_call(kernel, out_shape=(vmem((24, 2, 8, 128), F32), vmem((NV *...]
where the time goes in v1:
time: 27.8 us; the launch traced here: 27.7 us
  Pallas kernels  27.1 us (97%)
  between operations  0.64 us (2%)
    pallas_call x1, Pallas kernels, shards(): pl.pallas_call(kernel, out_shape=(vmem((24, 2, 8, 128), F32), vmem((NV *...  26.4 us
    pallas_call x1, Pallas kernels, shards(): pl.pallas_call(finish, out_shape=(jax.ShapeDtypeStruct((24, 2, 8, 128), F...  0.7 us

profile of v1, /device:TPU:1, one launch (start us, length us, event | category | flops | bytes accessed | tf_op | source)
XLA Modules:
  0.0 27.7 jit_solution(3574780223649367316)
XLA Ops:
  0.6 26.4 %smooth_and_restrict.1 = (f32[24,2,8,128]{3,2,1,0:T(8,128)S(1)}, f32[24,8,128]{2,1,0:T(8,128)S(1)}) custom-call(f32[24,2,8,128]{3,2,1,0:T(8,128)} %bitcast.20, bf16[4,2,9,16,128]{4,3,2,1,0:T(8,128)(2,1)} %bitcast.19, bf16[2,2,36,16,128]{4,3,2,1,0:T(8,128)(2,1)} %bitcast.18, bf16[192,48,128]{2,1,0:T(8,128)(2,1)} %bitcast.17, s32[8]{0:T(128)} %bitcast.21), custom_call_target="tpu_custom_call" | custom-call | tf_op jit(solution)/shard_map/smooth_and_restrict/pallas_call | solution.py:442
  27.0 0.7 %finish.1 = (f32[24,2,8,128]{3,2,1,0:T(8,128)}, f32[2,12,2,16]{3,2,1,0:T(2,128)}) custom-call(f32[24,2,8,128]{3,2,1,0:T(8,128)S(1)} %get-tuple-element.6.smooth, f32[24,8,128]{2,1,0:T(8,128)S(1)} %get-tuple-element.7.sums), custom_call_target="tpu_custom_call" | custom-call | tf_op jit(solution)/shard_map/finish/pallas_call | solution.py:474

commit v2 on v1

--- a/solution.py
+++ b/solution.py
@@ -90,7 +90,7 @@
     loads = [
         pltpu.make_async_copy(source, target, load_sem.at[i])
         for i, (source, target) in enumerate(
-            ((rs_hbm, rs), (clover_hbm, clover), (links_hbm, links16), (near_hbm, near), (owners_hbm, owners))
+            ((links_hbm, links16), (rs_hbm, rs), (clover_hbm, clover), (near_hbm, near), (owners_hbm, owners))
         )
     ]
     for copy in loads[:3] + loads[4:]:
@@ -184,7 +184,13 @@
     sums[...] = jnp.zeros(sums.shape, F32)
 
     loads[0].wait()
+    for order, (mu, _) in enumerate(CROSSING):
+        for part in range(2):
+            for at in range(9):
+                value = links16[mu, part, at].astype(F32).reshape(2, 8, 128)
+                face_links[order, part, at] = pack([value, value], mu, True)
     loads[1].wait()
+    loads[2].wait()
 
     def body(sweep, carry):
         kept = jnp.where(sweep == SWEEPS - 1, 1.0, 0.0)
@@ -210,12 +216,6 @@
 
         @pl.when(sweep == 0)
         def _():
-            loads[2].wait()
-            for order, (mu, _) in enumerate(CROSSING):
-                for part in range(2):
-                    for at in range(9):
-                        value = links16[mu, part, at].astype(F32).reshape(2, 8, 128)
-                        face_links[order, part, at] = pack([value, value], mu, True)
             pl.semaphore_wait(barrier, greeted)
 
         for order, (mu, axis) in enumerate(CROSSING):
@@ -224,7 +224,6 @@
                 for color in range(3):
                     outbox[sweep, 2 * order, part * 3 + color] = pack(
                         [half[0][color][part], half[1][color][part]], mu, False)
-            message(sweep, 2 * order, axis, -1).start()
         for order, (mu, axis) in enumerate(CROSSING):
             half = project(load_field, mu, 1)
             packed = [
@@ -239,6 +238,8 @@
                 pair = color_row(face_link, packed, row, True)
                 for part in range(2):
                     outbox[sweep, 2 * order + 1, part * 3 + row] = pair[part]
+        for order, (mu, axis) in enumerate(CROSSING):
+            message(sweep, 2 * order, axis, -1).start()
             message(sweep, 2 * order + 1, axis, 1).start()
 
         @pl.when(sweep == 0)
@@ -295,18 +296,18 @@
                             acc[at] = value
                 started = True
 
-        for order, (mu, axis) in enumerate(CROSSING):
+        for order, (mu, axis) in reversed(list(enumerate(CROSSING))):
             message(sweep, 2 * order, axis, -1).wait_recv()
             message(sweep, 2 * order + 1, axis, 1).wait_recv()
-        for row in range(3):
-            totals = [
-                [[acc[component(part, spin, row), side] for side in range(2)] for part in range(2)]
-                for spin in range(4)
-            ]
-            for order, (mu, axis) in enumerate(CROSSING):
-                def face_link(part, at_row, column, order=order):
-                    return face_links[order, part, at_row * 3 + column]
-
+
+            def face_link(part, at_row, column, order=order):
+                return face_links[order, part, at_row * 3 + column]
+
+            for row in range(3):
+                totals = [
+                    [[acc[component(part, spin, row), side] for side in range(2)] for part in range(2)]
+                    for spin in range(4)
+                ]
                 for sign in (-1, 1):
                     way = 2 * order + (0 if sign < 0 else 1)
                     if sign < 0:
@@ -329,10 +330,10 @@
                                 source, power = LOWER[mu][spin - 2]
                                 total = add_phase(base, pieces[source], power, sign)
                             totals[spin][0][side], totals[spin][1][side] = total
-            for spin in range(4):
-                for part in range(2):
-                    for side in range(2):
-                        acc[component(part, spin, row), side] = totals[spin][part][side]
+                for spin in range(4):
+                    for part in range(2):
+                        for side in range(2):
+                            acc[component(part, spin, row), side] = totals[spin][part][side]
         return carry
 
     lax.fori_loop(0, SWEEPS, body, 0)
@@ -345,49 +346,63 @@
                     at = ((part * 3 + color) * 2 + side) * 4 + spin
                     tiles[at * 8:(at + 1) * 8, :] = value[side]
     rows = jnp.concatenate([tiles[pl.ds(r, 48, stride=8), :] for r in range(8)], axis=0).astype(BF16)
-    placed = jnp.dot(rows, placing[...], preferred_element_type=F32)
+    mine = me["xy"]
+
+    def parcel(owner):
+        return pltpu.make_async_remote_copy(
+            src_ref=parcels.at[owner],
+            dst_ref=arrived.at[mine],
+            send_sem=parcel_send.at[owner],
+            recv_sem=parcel_recv.at[mine],
+            device_id={"xy": owner},
+            device_id_type=MESH,
+        )
+
+    lane = lax.broadcasted_iota(jnp.int32, (48, 128), 1) // 16
+    flags = {step: jnp.where((lane & step) != 0, 1.0, 0.0).astype(BF16) for step in (1, 2, 4)}
     for part in range(slots // 8):
-        parts = [placed[r * 48:(r + 1) * 48, part * 128:(part + 1) * 128] for r in range(8)]
-        lane = lax.broadcasted_iota(jnp.int32, (48, 128), 1) // 16
-        for step in (1, 2, 4):
+        placed = jnp.dot(rows, placing[:, part * 128:(part + 1) * 128], preferred_element_type=F32)
+        parts = [placed[r * 48:(r + 1) * 48, :].astype(BF16) for r in range(8)]
+        for step in (4, 2, 1):
             for r in range(8):
                 if r & step:
                     continue
                 first, second = parts[r], parts[r + step]
-                odd = (lane & step) != 0
+                odd = flags[step] > 0
                 parts[r] = jnp.where(odd, roll(second, step * 16, 1), first)
                 parts[r + step] = jnp.where(odd, second, roll(first, -step * 16, 1))
         for r in range(8):
             slot = part * 8 + r
-            parcels[slot // MOST, slot % MOST] = parts[r].astype(BF16)
-
-    def parcel(offset):
-        return pltpu.make_async_remote_copy(
-            src_ref=parcels.at[shifted("xy", offset)],
-            dst_ref=arrived.at[offset],
-            send_sem=parcel_send.at[offset],
-            recv_sem=parcel_recv.at[offset],
-            device_id={"xy": shifted("xy", offset)},
-            device_id_type=MESH,
-        )
-
-    for offset in sorted(range(1, groups), key=lambda o: -min(o, groups - o)):
-        parcel(offset).start()
-    arrived[0] = parcels[me["xy"]]
+            parcels[slot // MOST, slot % MOST] = parts[r]
+    for turn in sorted(range(1, groups), key=lambda o: -min(o, groups - o)):
+        parcel(lax.rem(mine + turn, groups)).start()
+
     loads[3].wait()
 
     def contract(index, carry):
-        half = (index + 1) // 2
-        offset = jnp.where(index % 2 == 1, half, lax.rem(groups - half, groups))
+        pair = index // 2
+        away = jnp.where(pair == 2, groups // 2 - 1, jnp.where(pair == 3, groups // 2 - 2, pair))
+        chip = lax.rem(mine // 2 + away, groups // 2)
+        source = chip * 2 + lax.rem(mine + index, 2)
 
         @pl.when(index > 0)
         def _():
-            parcel(offset).wait_recv()
-
-        source = lax.rem(me["xy"] - offset + groups, groups)
+            pltpu.make_async_remote_copy(
+                src_ref=parcels.at[source],
+                dst_ref=arrived.at[source],
+                send_sem=parcel_send.at[source],
+                recv_sem=parcel_recv.at[source],
+                device_id={"xy": source},
+                device_id_type=MESH,
+            ).wait_recv()
+
+        @pl.when(index == 0)
+        def _():
+            arrived[mine] = parcels[mine]
+
         for m in range(MOST):
             slot = source * MOST + m
-            tile = arrived[offset, m].astype(F32).reshape(6, 8, 128)
+            tile = arrived[source, m].astype(F32).reshape(6, 8, 128)
             turned = jnp.concatenate([tile[3:], -tile[:3]], axis=0)
             for v in range(NV):
                 vector = near[slot * NV + v].astype(F32).reshape(6, 8, 128)
@@ -401,8 +416,8 @@
         for order, (mu, axis) in enumerate(CROSSING):
             message(sweep, 2 * order, axis, -1).wait_send()
             message(sweep, 2 * order + 1, axis, 1).wait_send()
-    for offset in range(1, groups):
-        parcel(offset).wait_send()
+    for turn in range(1, groups):
+        parcel(lax.rem(mine + turn, groups)).wait_send()
 
 
 def finish(smooth, sums, smoothed, coarse, staged, sems):

time: 27.8 us -> 27.3 us (0.982)
  Pallas kernels: 27.1 us -> 26.6 us
    pallas_call x1, Pallas kernels: 26.4 us -> 25.9 us  [shards(): pl.pallas_call(kernel, out_shape=(vmem((24, 2, 8, 128), F32), vmem((NV *...]
where the time goes in v2:
time: 27.3 us; the launch traced here: 27.2 us
  Pallas kernels  26.6 us (97%)
  between operations  0.64 us (2%)
    pallas_call x1, Pallas kernels, shards(): pl.pallas_call(kernel, out_shape=(vmem((24, 2, 8, 128), F32), vmem((NV *...  25.9 us
    pallas_call x1, Pallas kernels, shards(): pl.pallas_call(finish, out_shape=(jax.ShapeDtypeStruct((24, 2, 8, 128), F...  0.7 us

profile of v2, /device:TPU:1, one launch (start us, length us, event | category | flops | bytes accessed | tf_op | source)
XLA Modules:
  0.0 27.2 jit_solution(1144506003744886034)
XLA Ops:
  0.6 25.9 %smooth_and_restrict.1 = (f32[24,2,8,128]{3,2,1,0:T(8,128)S(1)}, f32[24,8,128]{2,1,0:T(8,128)S(1)}) custom-call(f32[24,2,8,128]{3,2,1,0:T(8,128)} %bitcast.20, bf16[4,2,9,16,128]{4,3,2,1,0:T(8,128)(2,1)} %bitcast.19, bf16[2,2,36,16,128]{4,3,2,1,0:T(8,128)(2,1)} %bitcast.18, bf16[192,48,128]{2,1,0:T(8,128)(2,1)} %bitcast.17, s32[8]{0:T(128)} %bitcast.21), custom_call_target="tpu_custom_call" | custom-call | tf_op jit(solution)/shard_map/smooth_and_restrict/pallas_call | solution.py:457
  26.5 0.7 %finish.1 = (f32[24,2,8,128]{3,2,1,0:T(8,128)}, f32[2,12,2,16]{3,2,1,0:T(2,128)}) custom-call(f32[24,2,8,128]{3,2,1,0:T(8,128)S(1)} %get-tuple-element.6.smooth, f32[24,8,128]{2,1,0:T(8,128)S(1)} %get-tuple-element.7.sums), custom_call_target="tpu_custom_call" | custom-call | tf_op jit(solution)/shard_map/finish/pallas_call | solution.py:489

commit v3 on v2

--- a/solution.py
+++ b/solution.py
@@ -358,11 +358,11 @@
             device_id_type=MESH,
         )
 
+    placed = jnp.dot(rows, placing[...], preferred_element_type=F32)
     lane = lax.broadcasted_iota(jnp.int32, (48, 128), 1) // 16
     flags = {step: jnp.where((lane & step) != 0, 1.0, 0.0).astype(BF16) for step in (1, 2, 4)}
     for part in range(slots // 8):
-        placed = jnp.dot(rows, placing[:, part * 128:(part + 1) * 128], preferred_element_type=F32)
-        parts = [placed[r * 48:(r + 1) * 48, :].astype(BF16) for r in range(8)]
+        parts = [placed[r * 48:(r + 1) * 48, part * 128:(part + 1) * 128].astype(BF16) for r in range(8)]
         for step in (4, 2, 1):
             for r in range(8):
                 if r & step:
@@ -377,6 +377,10 @@
     for turn in sorted(range(1, groups), key=lambda o: -min(o, groups - o)):
         parcel(lax.rem(mine + turn, groups)).start()
 
+    for sweep in range(SWEEPS):
+        for order, (mu, axis) in enumerate(CROSSING):
+            message(sweep, 2 * order, axis, -1).wait_send()
+            message(sweep, 2 * order + 1, axis, 1).wait_send()
     loads[3].wait()
 
     def contract(index, carry):
@@ -412,10 +416,6 @@
         return carry
 
     lax.fori_loop(0, groups, contract, 0)
-    for sweep in range(SWEEPS):
-        for order, (mu, axis) in enumerate(CROSSING):
-            message(sweep, 2 * order, axis, -1).wait_send()
-            message(sweep, 2 * order + 1, axis, 1).wait_send()
     for turn in range(1, groups):
         parcel(lax.rem(mine + turn, groups)).wait_send()
 

time: 27.3 us -> 27.3 us (level)
  no operation moved by 1% of the time
where the time goes in v3:
time: 27.3 us; the launch traced here: 27.2 us
  Pallas kernels  26.6 us (97%)
  between operations  0.64 us (2%)
    pallas_call x1, Pallas kernels, shards(): pl.pallas_call(kernel, out_shape=(vmem((24, 2, 8, 128), F32), vmem((NV *...  25.9 us
    pallas_call x1, Pallas kernels, shards(): pl.pallas_call(finish, out_shape=(jax.ShapeDtypeStruct((24, 2, 8, 128), F...  0.7 us

profile of v3, /device:TPU:1, one launch (start us, length us, event | category | flops | bytes accessed | tf_op | source)
XLA Modules:
  0.0 27.2 jit_solution(18115609639468944550)
XLA Ops:
  0.6 25.9 %smooth_and_restrict.1 = (f32[24,2,8,128]{3,2,1,0:T(8,128)S(1)}, f32[24,8,128]{2,1,0:T(8,128)S(1)}) custom-call(f32[24,2,8,128]{3,2,1,0:T(8,128)} %bitcast.20, bf16[4,2,9,16,128]{4,3,2,1,0:T(8,128)(2,1)} %bitcast.19, bf16[2,2,36,16,128]{4,3,2,1,0:T(8,128)(2,1)} %bitcast.18, bf16[192,48,128]{2,1,0:T(8,128)(2,1)} %bitcast.17, s32[8]{0:T(128)} %bitcast.21), custom_call_target="tpu_custom_call" | custom-call | tf_op jit(solution)/shard_map/smooth_and_restrict/pallas_call | solution.py:457
  26.5 0.7 %finish.1 = (f32[24,2,8,128]{3,2,1,0:T(8,128)}, f32[2,12,2,16]{3,2,1,0:T(2,128)}) custom-call(f32[24,2,8,128]{3,2,1,0:T(8,128)S(1)} %get-tuple-element.6.smooth, f32[24,8,128]{2,1,0:T(8,128)S(1)} %get-tuple-element.7.sums), custom_call_target="tpu_custom_call" | custom-call | tf_op jit(solution)/shard_map/finish/pallas_call | solution.py:489

commit v4 on v3

--- a/solution.py
+++ b/solution.py
@@ -76,7 +76,7 @@
 
 
 def kernel(rs_hbm, links_hbm, clover_hbm, near_hbm, owners_hbm, smooth, sums,
-           rs, links16, clover, near, owners, links, face_links, field, acc,
+           rs, links16, clover, near, near32, owners, links, face_links, field, acc,
            outbox, inbox, tiles, placing, parcels, arrived,
            load_sem, send_sem, recv_sem, parcel_send, parcel_recv):
     groups = lax.axis_size("xy")
@@ -295,6 +295,17 @@
                         for at, value in zip(places, total):
                             acc[at] = value
                 started = True
+
+        @pl.when(sweep == 1)
+        def _():
+            loads[3].wait()
+
+            def widen(at, carry):
+                for v in range(NV):
+                    near32[at * NV + v] = near[at * NV + v].astype(F32).reshape(6, 8, 128)
+                return carry
+
+            lax.fori_loop(0, slots, widen, 0)
 
         for order, (mu, axis) in reversed(list(enumerate(CROSSING))):
             message(sweep, 2 * order, axis, -1).wait_recv()
@@ -381,8 +392,6 @@
         for order, (mu, axis) in enumerate(CROSSING):
             message(sweep, 2 * order, axis, -1).wait_send()
             message(sweep, 2 * order + 1, axis, 1).wait_send()
-    loads[3].wait()
-
     def contract(index, carry):
         pair = index // 2
         away = jnp.where(pair == 2, groups // 2 - 1, jnp.where(pair == 3, groups // 2 - 2, pair))
@@ -409,7 +418,7 @@
             tile = arrived[source, m].astype(F32).reshape(6, 8, 128)
             turned = jnp.concatenate([tile[3:], -tile[:3]], axis=0)
             for v in range(NV):
-                vector = near[slot * NV + v].astype(F32).reshape(6, 8, 128)
+                vector = near32[slot * NV + v]
                 for part, other in enumerate((tile, turned)):
                     total = jnp.sum(jnp.sum(vector * other, axis=0), axis=1, keepdims=True)
                     sums[v * 2 + part] = jnp.where(lane8 == slot, total, sums[v * 2 + part])
@@ -464,6 +473,7 @@
             vmem((4, 2, 9, 16, 128), BF16),
             vmem((2, 2, 36, 16, 128), BF16),
             vmem((slots * NV, 48, 128), BF16),
+            vmem((slots * NV, 6, 8, 128), F32),
             pltpu.SMEM((AGGS,), jnp.int32),
             vmem((4, 2, 9, 2, 8, 128), F32),
             vmem((3, 2, 9, 8, 128), F32),

time: 27.3 us -> 27.3 us (level)
  no operation moved by 1% of the time
where the time goes in v4:
time: 27.3 us; the launch traced here: 27.2 us
  Pallas kernels  26.5 us (97%)
  between operations  0.64 us (2%)
    pallas_call x1, Pallas kernels, shards(): pl.pallas_call(kernel, out_shape=(vmem((24, 2, 8, 128), F32), vmem((NV *...  25.8 us
    pallas_call x1, Pallas kernels, shards(): pl.pallas_call(finish, out_shape=(jax.ShapeDtypeStruct((24, 2, 8, 128), F...  0.7 us

profile of v4, /device:TPU:1, one launch (start us, length us, event | category | flops | bytes accessed | tf_op | source)
XLA Modules:
  0.0 27.2 jit_solution(4776737546470454655)
XLA Ops:
  0.6 25.8 %smooth_and_restrict.1 = (f32[24,2,8,128]{3,2,1,0:T(8,128)S(1)}, f32[24,8,128]{2,1,0:T(8,128)S(1)}) custom-call(f32[24,2,8,128]{3,2,1,0:T(8,128)} %bitcast.20, bf16[4,2,9,16,128]{4,3,2,1,0:T(8,128)(2,1)} %bitcast.19, bf16[2,2,36,16,128]{4,3,2,1,0:T(8,128)(2,1)} %bitcast.18, bf16[192,48,128]{2,1,0:T(8,128)(2,1)} %bitcast.17, s32[8]{0:T(128)} %bitcast.21), custom_call_target="tpu_custom_call" | custom-call | tf_op jit(solution)/shard_map/smooth_and_restrict/pallas_call | solution.py:466
  26.5 0.7 %finish.1 = (f32[24,2,8,128]{3,2,1,0:T(8,128)}, f32[2,12,2,16]{3,2,1,0:T(2,128)}) custom-call(f32[24,2,8,128]{3,2,1,0:T(8,128)S(1)} %get-tuple-element.6.smooth, f32[24,8,128]{2,1,0:T(8,128)S(1)} %get-tuple-element.7.sums), custom_call_target="tpu_custom_call" | custom-call | tf_op jit(solution)/shard_map/finish/pallas_call | solution.py:499

commit v5 on v3

--- a/solution.py
+++ b/solution.py
@@ -410,9 +410,11 @@
             turned = jnp.concatenate([tile[3:], -tile[:3]], axis=0)
             for v in range(NV):
                 vector = near[slot * NV + v].astype(F32).reshape(6, 8, 128)
-                for part, other in enumerate((tile, turned)):
-                    total = jnp.sum(jnp.sum(vector * other, axis=0), axis=1, keepdims=True)
-                    sums[v * 2 + part] = jnp.where(lane8 == slot, total, sums[v * 2 + part])
+                real, imaginary = (jnp.sum(vector * other, axis=0) for other in (tile, turned))
+                both = jnp.where(upper_rows, imaginary, real)
+                both = both + roll(jnp.where(upper_rows, real, imaginary), 4, 0)
+                total = jnp.sum(both, axis=1, keepdims=True)
+                sums[v] = jnp.where(lane8 == slot, total, sums[v])
         return carry
 
     lax.fori_loop(0, groups, contract, 0)
@@ -425,11 +427,10 @@
     first.start()
     slots = coarse.shape[-1]
     total = sums[...]
-    total = total + roll(total, 4, 1)
     total = total + roll(total, -1, 1)
-    total = total.reshape(NV, 2, 8, 128)
     for chirality in range(2):
-        staged[chirality] = total[:, :, 2 * chirality, :slots]
+        for part in range(2):
+            staged[chirality, :, part] = total[:, 4 * part + 2 * chirality, :slots]
     second = pltpu.make_async_copy(staged, coarse, sems.at[1])
     second.start()
     first.wait()
@@ -456,7 +457,7 @@
     ]
     smooth, sums = pl.pallas_call(
         kernel,
-        out_shape=(vmem((24, 2, 8, 128), F32), vmem((NV * 2, 8, 128), F32)),
+        out_shape=(vmem((24, 2, 8, 128), F32), vmem((NV, 8, 128), F32)),
         in_specs=[anywhere] * 5,
         out_specs=(inside, inside),
         scratch_shapes=[

time: 27.3 us -> 27.3 us (level)
  no operation moved by 1% of the time
where the time goes in v5:
time: 27.3 us; the launch traced here: 27.2 us
  Pallas kernels  26.6 us (97%)
  between operations  0.64 us (2%)
    pallas_call x1, Pallas kernels, shards(): pl.pallas_call(kernel, out_shape=(vmem((24, 2, 8, 128), F32), vmem((NV, 8...  25.9 us
    pallas_call x1, Pallas kernels, shards(): pl.pallas_call(finish, out_shape=(jax.ShapeDtypeStruct((24, 2, 8, 128), F...  0.7 us

profile of v5, /device:TPU:1, one launch (start us, length us, event | category | flops | bytes accessed | tf_op | source)
XLA Modules:
  0.0 27.2 jit_solution(6832021741159872515)
XLA Ops:
  0.6 25.9 %smooth_and_restrict.1 = (f32[24,2,8,128]{3,2,1,0:T(8,128)S(1)}, f32[12,8,128]{2,1,0:T(8,128)S(1)}) custom-call(f32[24,2,8,128]{3,2,1,0:T(8,128)} %bitcast.20, bf16[4,2,9,16,128]{4,3,2,1,0:T(8,128)(2,1)} %bitcast.19, bf16[2,2,36,16,128]{4,3,2,1,0:T(8,128)(2,1)} %bitcast.18, bf16[192,48,128]{2,1,0:T(8,128)(2,1)} %bitcast.17, s32[8]{0:T(128)} %bitcast.21), custom_call_target="tpu_custom_call" | custom-call | tf_op jit(solution)/shard_map/smooth_and_restrict/pallas_call | solution.py:458
  26.5 0.7 %finish.1 = (f32[24,2,8,128]{3,2,1,0:T(8,128)}, f32[2,12,2,16]{3,2,1,0:T(2,128)}) custom-call(f32[24,2,8,128]{3,2,1,0:T(8,128)S(1)} %get-tuple-element.6.smooth, f32[12,8,128]{2,1,0:T(8,128)S(1)} %get-tuple-element.7.sums), custom_call_target="tpu_custom_call" | custom-call | tf_op jit(solution)/shard_map/finish/pallas_call | solution.py:490

commit v6 on v3

--- a/solution.py
+++ b/solution.py
@@ -76,8 +76,8 @@
 
 
 def kernel(rs_hbm, links_hbm, clover_hbm, near_hbm, owners_hbm, smooth, sums,
-           rs, links16, clover, near, owners, links, face_links, field, acc,
-           outbox, inbox, tiles, placing, parcels, arrived,
+           rs, links16, clover, near, owners, links, face_links, field, hops,
+           outbox, inbox, placing, parcels, arrived,
            load_sem, send_sem, recv_sem, parcel_send, parcel_recv):
     groups = lax.axis_size("xy")
     slots = groups * MOST
@@ -169,6 +169,17 @@
     def load_field(spin, color):
         return field[component(0, spin, color)], field[component(1, spin, color)]
 
+    def hop_rows(part, spin, color, side):
+        at = ((part * 3 + color) * 2 + side) * 4 + spin
+        return slice(at * 8, (at + 1) * 8)
+
+    def load_hop(part, spin, color):
+        return jnp.stack([hops[hop_rows(part, spin, color, side), :] for side in range(2)])
+
+    def store_hop(part, spin, color, value):
+        for side in range(2):
+            hops[hop_rows(part, spin, color, side), :] = value[side]
+
     def message(sweep, way, axis, offset):
         return pltpu.make_async_remote_copy(
             src_ref=outbox.at[sweep, way],
@@ -179,7 +190,7 @@
             device_id_type=MESH,
         )
 
-    acc[...] = jnp.zeros(acc.shape, F32)
+    hops[...] = jnp.zeros(hops.shape, F32)
     smooth[...] = jnp.zeros(smooth.shape, F32)
     sums[...] = jnp.zeros(sums.shape, F32)
 
@@ -196,7 +207,7 @@
         kept = jnp.where(sweep == SWEEPS - 1, 1.0, 0.0)
         for chirality in range(2):
             vector = [
-                [rs[component(part, 2 * chirality, j)] + HOPPING * acc[component(part, 2 * chirality, j)]
+                [rs[component(part, 2 * chirality, j)] + HOPPING * load_hop(part, 2 * chirality + j // 3, j % 3)
                  for part in range(2)]
                 for j in range(6)
             ]
@@ -285,15 +296,14 @@
                             pair = tuple(neighbour(value, mu, False) for value in pair)
                         moved.append(pair)
                     for spin in range(4):
-                        places = [component(part, spin, row) for part in range(2)]
-                        base = tuple(acc[at] for at in places) if started else (0.0, 0.0)
+                        base = tuple(load_hop(part, spin, row) for part in range(2)) if started else (0.0, 0.0)
                         if spin < 2:
                             total = add_phase(base, moved[spin], 0, 1)
                         else:
                             source, power = LOWER[mu][spin - 2]
                             total = add_phase(base, moved[source], power, sign)
-                        for at, value in zip(places, total):
-                            acc[at] = value
+                        for part, value in enumerate(total):
+                            store_hop(part, spin, row, value)
                 started = True
 
         for order, (mu, axis) in reversed(list(enumerate(CROSSING))):
@@ -305,7 +315,7 @@
 
             for row in range(3):
                 totals = [
-                    [[acc[component(part, spin, row), side] for side in range(2)] for part in range(2)]
+                    [[hops[hop_rows(part, spin, row, side), :] for side in range(2)] for part in range(2)]
                     for spin in range(4)
                 ]
                 for sign in (-1, 1):
@@ -333,19 +343,13 @@
                 for spin in range(4):
                     for part in range(2):
                         for side in range(2):
-                            acc[component(part, spin, row), side] = totals[spin][part][side]
+                            hops[hop_rows(part, spin, row, side), :] = totals[spin][part][side]
         return carry
 
     lax.fori_loop(0, SWEEPS, body, 0)
 
-    for part in range(2):
-        for color in range(3):
-            for spin in range(4):
-                value = HOPPING * acc[component(part, spin, color)]
-                for side in range(2):
-                    at = ((part * 3 + color) * 2 + side) * 4 + spin
-                    tiles[at * 8:(at + 1) * 8, :] = value[side]
-    rows = jnp.concatenate([tiles[pl.ds(r, 48, stride=8), :] for r in range(8)], axis=0).astype(BF16)
+    residual = [HOPPING * hops[pl.ds(r, 48, stride=8), :] for r in range(8)]
+    rows = jnp.concatenate(residual, axis=0).astype(BF16)
     mine = me["xy"]
 
     def parcel(owner):
@@ -468,10 +472,9 @@
             vmem((4, 2, 9, 2, 8, 128), F32),
             vmem((3, 2, 9, 8, 128), F32),
             vmem((24, 2, 8, 128), F32),
-            vmem((24, 2, 8, 128), F32),
+            vmem((384, 128), F32),
             vmem((SWEEPS, 6, 6, 8, 128), F32),
             vmem((SWEEPS, 6, 6, 8, 128), F32),
-            vmem((384, 128), F32),
             vmem((128, slots * 16), BF16),
             vmem((groups, MOST, 48, 128), BF16),
             vmem((groups, MOST, 48, 128), BF16),

time: 27.3 us -> 27.3 us (level)
  no operation moved by 1% of the time
where the time goes in v6:
time: 27.3 us; the launch traced here: 27.2 us
  Pallas kernels  26.6 us (97%)
  between operations  0.64 us (2%)
    pallas_call x1, Pallas kernels, shards(): pl.pallas_call(kernel, out_shape=(vmem((24, 2, 8, 128), F32), vmem((NV *...  25.9 us
    pallas_call x1, Pallas kernels, shards(): pl.pallas_call(finish, out_shape=(jax.ShapeDtypeStruct((24, 2, 8, 128), F...  0.7 us

profile of v6, /device:TPU:1, one launch (start us, length us, event | category | flops | bytes accessed | tf_op | source)
XLA Modules:
  0.0 27.2 jit_solution(964052868694831202)
XLA Ops:
  0.6 25.9 %smooth_and_restrict.1 = (f32[24,2,8,128]{3,2,1,0:T(8,128)S(1)}, f32[24,8,128]{2,1,0:T(8,128)S(1)}) custom-call(f32[24,2,8,128]{3,2,1,0:T(8,128)} %bitcast.20, bf16[4,2,9,16,128]{4,3,2,1,0:T(8,128)(2,1)} %bitcast.19, bf16[2,2,36,16,128]{4,3,2,1,0:T(8,128)(2,1)} %bitcast.18, bf16[192,48,128]{2,1,0:T(8,128)(2,1)} %bitcast.17, s32[8]{0:T(128)} %bitcast.21), custom_call_target="tpu_custom_call" | custom-call | tf_op jit(solution)/shard_map/smooth_and_restrict/pallas_call | solution.py:461
  26.5 0.7 %finish.1 = (f32[24,2,8,128]{3,2,1,0:T(8,128)}, f32[2,12,2,16]{3,2,1,0:T(2,128)}) custom-call(f32[24,2,8,128]{3,2,1,0:T(8,128)S(1)} %get-tuple-element.6.smooth, f32[24,8,128]{2,1,0:T(8,128)S(1)} %get-tuple-element.7.sums), custom_call_target="tpu_custom_call" | custom-call | tf_op jit(solution)/shard_map/finish/pallas_call | solution.py:492
